TPU v7x, 256 devices: a whole 4x4x8 slice. The times are simulated.
256 devices in a mesh: gx: 32 (over x, z_lo, core), gy: 8 (over z_hi, y).
Axes of the slice: x: 4, y: 4, z: 8 (z_hi: 2, z_lo: 4; z = z_hi * 4 + z_lo), core: 2. Of those that a mesh axis runs over, the one named last changes fastest.
Arguments:
- tracers: float32 [2, 16, 384, 4096], P(None, None, 'gy', 'gx'), may hold values from -6 to 6
- east_speed: float32 [16, 384, 4096], P(None, 'gy', 'gx'), may hold values from -0.45 to 0.45
- north_speed: float32 [16, 384, 4096], P(None, 'gy', 'gx'), may hold values from -0.45 to 0.45
- bottom_level: int32 [384, 4096], P('gy', 'gx'), may hold values from 0 to 16
Outputs:
- stepped: float32 [2, 16, 384, 4096], P(None, None, 'gy', 'gx')
Inputs may be any that keep to these rules, and one draw needn't show every extreme that they name: Level k of a column is water where k < bottom_level, land otherwise.
All inputs are finite; a program needn't handle non-finite values.
Results may differ from a plain program's by a relative error of at most 0.0003.
Values sent between devices are 32-bit elements; how exact they have to be, the bound alone decides.
A program may use at most 64 MiB of HBM per device.

v0:
```python
import functools

import jax
import jax.numpy as jnp
from jax import lax
from jax.experimental import pallas as pl
from jax.experimental.pallas import tpu as pltpu
from jax.sharding import PartitionSpec as P

MESH = pl.DeviceIdType.MESH
NT, NZ, CY, CX = 2, 16, 48, 128
PAD = 8
TALL = CY + 2 * PAD
OCTETS = CY // 8
FOLD_ROWS = 72
OWN_LAST, FROM_NORTH, FROM_SOUTH, OWN_FIRST = (pl.ds(i, 2) for i in (0, 2, 4, 6))
PACKED = 13
EASTWARD = 6
WESTWARD = 5
BLOCK = 8
HEAT = 0.4
SALT = 0.6


def reciprocal(value):
    guess = pl.reciprocal(value, approx=True)
    return guess * (2.0 - value * guess)


def minmod(first, second):
    return jnp.maximum(jnp.minimum(first, second), 0.0) + jnp.minimum(
        jnp.maximum(first, second), 0.0
    )


def density(pair):
    return SALT * pair[1] - HEAT * pair[0]


def face_fluxes(local, before, after, dz_sum, speed):
    slope = jnp.clip(
        (0.1 * density(local)) * reciprocal(jnp.maximum(density(dz_sum), 1.0)), -0.025, 0.025
    )
    size = jnp.abs(speed)
    limited = 0.5 * size * (1.0 - size)
    forward = speed >= 0.0
    linear = jnp.minimum(speed, 0.0) - 0.1
    low, high, second = [], [], []
    for t in range(NT):
        correction = limited * minmod(local[t], jnp.where(forward, before[t], after[t]))
        taken = correction + (linear * local[t] + slope * dz_sum[t])
        low.append(taken)
        high.append(taken - speed * local[t])
        second.append(correction)
    return low, high, second, forward


def lanes_left(value):
    return pltpu.roll(value, CX - 1, 1)


def lanes_right(value):
    return pltpu.roll(value, 1, 1)


def rows_up(value):
    return pltpu.roll(value, 7, 0)


def rows_down(value):
    return pltpu.roll(value, 1, 0)


def edge_terms(field, dz, bottom, speed, level, nxt, prv, low_at, high_at, low_second, high_second):
    wet = jnp.minimum(bottom, nxt(bottom)) > level
    local = [jnp.where(wet, nxt(f) - f, 0.0) for f in field]
    dz_sum = [z + nxt(z) for z in dz]
    masked = jnp.where(wet, speed, 0.0)
    low, high, second, forward = face_fluxes(
        local, [prv(d) for d in local], [nxt(d) for d in local], dz_sum, masked
    )
    zero = jnp.zeros_like(masked)
    terms, steps = [], []
    for t in range(NT):
        late = zero
        if low_second is not None:
            late = late + jnp.where(low_second & ~forward, second[t], 0.0)
        if high_second is not None:
            late = late + jnp.where(high_second & forward, second[t], 0.0)
        arriving, term, step = late, -late, zero
        if high_at is not None:
            arriving = arriving + jnp.where(high_at, high[t], 0.0)
            step = step + prv(jnp.where(high_at, local[t], 0.0))
        if low_at is not None:
            term = term - jnp.where(low_at, low[t], 0.0)
            step = step + jnp.where(low_at, local[t], 0.0)
        terms.append(term + prv(arriving))
        steps.append(step)
    return terms, steps


def kernel(
    n_gx, n_gy,
    tracers, east, north, bottom, out,
    T, U, V, bottom_int, bf, be, bn, TZ, XY, YB, GX, GY, FY, Q,
    packed, to_east, to_west, from_west, from_east, relay, relay_b, relay_v, folded,
    strip, strip_b, strip_v, edge_c, edge_g,
    load_sem, send_sem, recv_sem, go_sem, go_north_sem,
):
    gx, gy = lax.axis_index("gx"), lax.axis_index("gy")
    east_id = (lax.rem(gx + 1, n_gx), gy)
    west_id = (lax.rem(gx + n_gx - 1, n_gx), gy)
    north_id = (gx, gy + 1)
    south_id = (gx, gy - 1)
    mirror_id = (n_gx - 1 - gx, gy)
    top = gy == n_gy - 1
    base = gy == 0
    below_middle = gy == n_gy // 2 - 1
    above_middle = gy == n_gy // 2
    place = lax.rem(gx, BLOCK)
    by_go = gy <= n_gy // 2
    after_seam = (place == 0) & by_go
    before_seam = (place == BLOCK - 1) & by_go
    crosses_down = place == BLOCK - 1
    crosses_up = crosses_down | ((lax.rem(place, 2) == 0) & (place != BLOCK - 2))
    relayed_up = crosses_up & below_middle
    relayed_down = crosses_down & above_middle
    relays_up = below_middle & jnp.logical_not(crosses_up)
    relays_down = (place == BLOCK - 2) & above_middle
    chip_mate = gx + 1 - 2 * lax.rem(gx, 2)

    barrier = pltpu.get_barrier_semaphore()

    def greet(device):
        pl.semaphore_signal(barrier, inc=1, device_id=device, device_id_type=MESH)

    pl.when(top)(lambda: greet(mirror_id))
    above_go = gy == n_gy // 2 + 1
    mate_sends_down = crosses_down & below_middle
    mate_sends_up = crosses_up & above_middle
    pl.when(mate_sends_down)(lambda: greet((chip_mate, gy + 1)))
    pl.when(mate_sends_up)(lambda: greet((chip_mate, gy - 1)))
    pl.when(jnp.logical_not(top | mate_sends_down))(lambda: greet(north_id))
    pl.when(jnp.logical_not(base | mate_sends_up | above_go))(lambda: greet(south_id))
    greet(west_id)
    pl.when(jnp.logical_not(before_seam))(lambda: greet(east_id))
    expected = (
        4 + (relays_up | relays_down).astype(jnp.int32) - (relayed_up | relayed_down).astype(jnp.int32)
        - after_seam.astype(jnp.int32) - base.astype(jnp.int32) - above_middle.astype(jnp.int32)
    )

    def load(source, target, index):
        copy = pltpu.make_async_copy(source, target, load_sem.at[index])
        copy.start()
        return copy

    last_rows, first_rows = pl.ds(CY - 2, 2), pl.ds(0, 2)
    early = [
        load(tracers.at[:, :, last_rows, :], strip.at[:, :, OWN_LAST, :], 0),
        load(tracers.at[:, :, first_rows, :], strip.at[:, :, OWN_FIRST, :], 1),
        load(bottom.at[last_rows, :], strip_b.at[OWN_LAST, :], 2),
        load(bottom.at[first_rows, :], strip_b.at[OWN_FIRST, :], 3),
        load(north.at[:, last_rows, :], strip_v.at[:, OWN_LAST, :], 4),
        load(north.at[:, first_rows, :], strip_v.at[:, OWN_FIRST, :], 5),
    ]
    late = [
        load(tracers, T.at[:, :, pl.ds(PAD, CY), :], 6),
        load(bottom, bottom_int, 7),
        load(east, U, 8),
        load(north, V, 9),
    ]

    lane = lax.broadcasted_iota(jnp.int32, (8, CX), 1)
    row = lax.broadcasted_iota(jnp.int32, (8, CX), 0)
    zeros = jnp.zeros((8, CX), jnp.float32)

    def octet(o):
        return pl.ds(PAD + 8 * o, 8)

    def shifted(o, by):
        return pl.ds(PAD + 8 * o + by, 8)

    for pad in (pl.ds(0, PAD), pl.ds(PAD + CY, PAD)):
        bf[pad, :] = zeros
        bn[pad, :] = zeros

    def clear(k, carry):
        for t in range(NT):
            YB[t, k, pl.ds(0, PAD), :] = zeros
            TZ[t, k, pl.ds(PAD + CY, PAD), :] = zeros
        return carry

    lax.fori_loop(0, NZ, clear, 0)

    @pl.when(base)
    def _():
        strip_b[FROM_SOUTH, :] = jnp.zeros((2, CX), jnp.int32)
        for t in range(NT):
            for k in range(NZ):
                strip[t, k, FROM_SOUTH, :] = jnp.zeros((2, CX), jnp.float32)

    for copy in early:
        copy.wait()

    def send(source, target, index, slot, device):
        return pltpu.make_async_remote_copy(
            src_ref=source, dst_ref=target, send_sem=send_sem.at[index], recv_sem=recv_sem.at[slot],
            device_id=device, device_id_type=MESH,
        )

    def bundle(sources, targets, index, slot, device):
        pairs = enumerate(zip(sources, targets, strict=True))
        return [send(source, target, index + i, slot + i, device) for i, (source, target) in pairs]

    def start(copies):
        for copy in copies:
            copy.start()

    def wait_recv(copies):
        for copy in copies:
            copy.wait_recv()

    def wait_send(copies):
        for copy in copies:
            copy.wait_send()

    eastward = send(to_east, from_west, 0, 0, east_id)
    westward = send(to_west, from_east, 1, 1, west_id)
    last = [strip.at[:, :, OWN_LAST, :], strip_b.at[OWN_LAST, :], strip_v.at[:, pl.ds(1, 1), :]]
    first = [strip.at[:, :, OWN_FIRST, :], strip_b.at[OWN_FIRST, :]]
    from_south = [strip.at[:, :, FROM_SOUTH, :], strip_b.at[FROM_SOUTH, :], strip_v.at[:, pl.ds(5, 1), :]]
    from_north = [strip.at[:, :, FROM_NORTH, :], strip_b.at[FROM_NORTH, :]]
    between = [relay, relay_b, relay_v]
    northward = bundle(last, from_south, 2, 2, north_id)
    southward = bundle(first, from_north, 5, 5, south_id)
    across = bundle(last[:2], from_north, 2, 5, mirror_id)
    handed_up = bundle(last, between, 2, 7, (chip_mate, gy))
    handed_down = bundle(first, between[:2], 5, 7, (chip_mate, gy))
    forwarded_up = bundle(between, from_south, 7, 2, (chip_mate, gy + 1))
    forwarded_down = bundle(between[:2], from_north, 7, 5, (chip_mate, gy - 1))
    northward_itself = jnp.logical_not(top | relayed_up)
    southward_itself = jnp.logical_not(base | relayed_down)
    even = lax.rem(gx, 2) == 0
    late_entry = below_middle & jnp.logical_not(relayed_up) & (place < BLOCK - 2)

    @pl.when(jnp.logical_not(late_entry))
    def _():
        pl.semaphore_wait(barrier, expected)

        @pl.when(before_seam)
        def _():
            pl.semaphore_signal(go_sem, inc=1, device_id=east_id, device_id_type=MESH)

        @pl.when(above_go)
        def _():
            pl.semaphore_signal(go_north_sem, inc=1, device_id=south_id, device_id_type=MESH)

        pl.when(relayed_up)(lambda: start(handed_up))

        @pl.when(relays_up)
        def _():
            wait_recv(handed_up)
            start(forwarded_up)

        pl.when(northward_itself & below_middle)(lambda: start(northward))
        pl.when(relayed_down)(lambda: start(handed_down))
        pl.when(southward_itself & jnp.logical_not(relays_down))(lambda: start(southward))
        pl.when(northward_itself & jnp.logical_not(below_middle | above_middle))(lambda: start(northward))
        pl.when(top)(lambda: start(across))

        @pl.when(relays_down)
        def _():
            wait_recv(handed_down)
            start(forwarded_down)
            start(southward)

    def send_columns():
        pl.when(jnp.logical_not(even))(eastward.start)
        pl.when(jnp.logical_not(after_seam))(westward.start)
        pl.when(even)(eastward.start)

    for copy in late[:3]:
        copy.wait()

    for o in range(OCTETS):
        bf[octet(o), :] = bottom_int[pl.ds(8 * o, 8), :].astype(jnp.float32)
    for o in range(OCTETS):
        here = bf[octet(o), :]
        be[octet(o), :] = jnp.where(lane == CX - 1, 0.0, jnp.minimum(here, lanes_left(here)))
        bn[octet(o), :] = jnp.minimum(here, bf[shifted(o, 1), :])

    slot_of = lane // 4

    def pack(group, carry):
        t0, t1, speed = zeros, zeros, zeros
        for b in range(4):
            for o in range(OCTETS):
                slot = b * 8 + o
                here = slot_of == slot
                shift = (4 * slot + 2) % CX
                k = 4 * group + b
                t0 = jnp.where(here, pltpu.roll(T[0, k, octet(o), :], shift, 1), t0)
                t1 = jnp.where(here, pltpu.roll(T[1, k, octet(o), :], shift, 1), t1)
                speed = jnp.where(here, pltpu.roll(U[k, pl.ds(8 * o, 8), :], shift, 1), speed)
        packed[group] = t0
        packed[4 + group] = t1
        packed[8 + group] = speed
        return carry

    lax.fori_loop(0, 4, pack, 0, unroll=4)
    packed_b = zeros
    for b in range(4):
        for o in range(OCTETS):
            slot = b * 8 + o
            packed_b = jnp.where(
                slot_of == slot, pltpu.roll(bf[octet(o), :], (4 * slot + 2) % CX, 1), packed_b
            )
    packed[12] = packed_b

    first_half = lax.rem(lane, 4) < 2
    east_speeds = zeros
    for j in range(4):
        to_east[j] = jnp.where(first_half, packed[j], pltpu.roll(packed[4 + j], 2, 1))
        to_west[j] = jnp.where(first_half, pltpu.roll(packed[4 + j], CX - 2, 1), packed[j])
        east_speeds = jnp.where(
            lax.rem(lane, 4) == j, pltpu.roll(packed[8 + j], (CX + j - 1) % CX, 1), east_speeds
        )
    to_east[4] = east_speeds
    to_east[5] = packed_b
    to_west[4] = packed_b

    pl.when(jnp.logical_not(late_entry))(send_columns)


    late[3].wait()

    def vertical(k, carry):
        level = k.astype(jnp.float32)
        above = jnp.where(k > 0, level, 99.0)
        down, up = jnp.minimum(k + 1, NZ - 1), jnp.maximum(k - 1, 0)
        for o in range(OCTETS):
            depth = bf[octet(o), :]
            for t in range(NT):
                here = T[t, k, octet(o), :]
                TZ[t, k, octet(o), :] = jnp.where(
                    depth > level + 1.0, T[t, down, octet(o), :] - here, 0.0
                ) + jnp.where(depth > above, here - T[t, up, octet(o), :], 0.0)
        return carry

    lax.fori_loop(0, NZ, vertical, 0, unroll=2)

    def inside(k, carry):
        level = k.astype(jnp.float32)
        for o in range(OCTETS):
            here = [T[t, k, octet(o), :] for t in range(NT)]
            dz = [TZ[t, k, octet(o), :] for t in range(NT)]
            wet = be[octet(o), :] > level
            local = [jnp.where(wet, lanes_left(f) - f, 0.0) for f in here]
            before = [lanes_right(d) for d in local]
            after = [lanes_left(d) for d in local]
            speed = jnp.where(wet, U[k, pl.ds(8 * o, 8), :], 0.0)
            low, high, _, _ = face_fluxes(
                local, before, after, [z + lanes_left(z) for z in dz], speed
            )
            across_x = [lanes_right(high[t]) - low[t] for t in range(NT)]
            for t in range(NT):
                GX[t, k, octet(o), :] = local[t] + before[t]

            wet = bn[octet(o), :] > level
            wet_before = bn[shifted(o, -1), :] > level
            wet_after = bn[shifted(o, 1), :] > level
            nxt = [T[t, k, shifted(o, 1), :] for t in range(NT)]
            local = [jnp.where(wet, nxt[t] - here[t], 0.0) for t in range(NT)]
            before = [
                jnp.where(wet_before, here[t] - T[t, k, shifted(o, -1), :], 0.0) for t in range(NT)
            ]
            after = [
                jnp.where(wet_after, T[t, k, shifted(o, 2), :] - nxt[t], 0.0) for t in range(NT)
            ]
            speed = jnp.where(wet, V[k, pl.ds(8 * o, 8), :], 0.0)
            low, high, _, _ = face_fluxes(
                local, before, after, [dz[t] + TZ[t, k, shifted(o, 1), :] for t in range(NT)], speed
            )
            for t in range(NT):
                GY[t, k, octet(o), :] = local[t] + before[t]
                XY[t, k, octet(o), :] = across_x[t] - low[t]
                YB[t, k, octet(o), :] = high[t]
        return carry

    lax.fori_loop(0, NZ, inside, 0, unroll=2)

    @pl.when(late_entry)
    def _():
        pl.semaphore_wait(barrier, expected)

        @pl.when(relays_up)
        def _():
            wait_recv(handed_up)
            start(forwarded_up)

        start(northward)
        send_columns()
        start(southward)

    @pl.when(above_middle)
    def _():
        pl.semaphore_wait(go_north_sem, 1)
        start(northward)

    @pl.when(after_seam)
    def _():
        pl.semaphore_wait(go_sem, 1)
        westward.start()

    def prepare(octets):
        def body(k, carry):
            level = k.astype(jnp.float32)
            down = jnp.minimum(k + 1, NZ - 1)
            for o in octets:
                open_below = bf[octet(o), :] > level + 1.0
                here = [T[t, k, octet(o), :] for t in range(NT)]
                step = [T[t, down, octet(o), :] - here[t] for t in range(NT)]
                mean_y = [GY[t, k, octet(o), :] + GY[t, down, octet(o), :] for t in range(NT)]
                inverse = jnp.where(
                    open_below, reciprocal(jnp.maximum(4.0 * density(step), 1.0)), 0.0
                )
                slope = jnp.clip(density(mean_y) * inverse, -1.0, 1.0)
                square = 0.1 * (slope * slope)
                slope = 0.025 * slope
                Q[k, octet(o), :] = inverse
                for t in range(NT):
                    FY[t, k, octet(o), :] = square * step[t] - slope * mean_y[t]
                    XY[t, k, octet(o), :] += here[t] + YB[t, k, shifted(o, -1), :]
            return carry

        lax.fori_loop(0, NZ, body, 0, unroll=2)

    inner, outer = tuple(range(1, OCTETS - 1)), (0, OCTETS - 1)
    prepare(inner)

    def edge_rows_in():
        wait_recv(southward)
        pl.when(jnp.logical_not(base))(lambda: wait_recv(northward))

        @pl.when(top)
        def _():
            def gather(k, carry):
                for t in range(NT):
                    folded[pl.ds(2 * (NZ * t + k), 2), :] = strip[t, k, FROM_NORTH, :]
                return carry

            def scatter(k, carry):
                for t in range(NT):
                    strip[t, k, FROM_NORTH, :] = folded[pl.ds(2 * (NZ * t + k), 2), :]
                return carry

            lax.fori_loop(0, NZ, gather, 0, unroll=4)
            folded[pl.ds(64, 8), :] = strip_b[...].astype(jnp.float32)
            for i in range(FOLD_ROWS // 8):
                value = folded[pl.ds(8 * i, 8), :]
                for bit in (64, 32, 16, 8, 4, 2, 1):
                    value = jnp.where(
                        (lane & bit) != 0, pltpu.roll(value, bit, 1), pltpu.roll(value, CX - bit, 1)
                    )
                folded[pl.ds(8 * i, 8), :] = jnp.where(
                    (row & 1) != 0, rows_down(value), rows_up(value)
                )
            lax.fori_loop(0, NZ, scatter, 0, unroll=4)
            strip_b[FROM_NORTH, :] = folded[pl.ds(66, 2), :].astype(jnp.int32)

        def edge_rows(k, carry):
            level = k.astype(jnp.float32)
            above = jnp.where(k > 0, level, 99.0)
            down, up = jnp.minimum(k + 1, NZ - 1), jnp.maximum(k - 1, 0)
            depth = strip_b[...].astype(jnp.float32)
            here = [strip[t, k] for t in range(NT)]
            dz = [
                jnp.where(depth > level + 1.0, strip[t, down] - here[t], 0.0)
                + jnp.where(depth > above, here[t] - strip[t, up], 0.0)
                for t in range(NT)
            ]
            terms, grads = edge_terms(
                here, dz, depth, strip_v[k], level, rows_up, rows_down,
                row == 1, row == 5, row == 0, row == 6,
            )
            for t in range(NT):
                XY[t, k, octet(0), :] += jnp.where(row < 2, pltpu.roll(terms[t], 2, 0), 0.0)
                GY[t, k, octet(0), :] += jnp.where(row < 2, pltpu.roll(grads[t], 2, 0), 0.0)
                XY[t, k, octet(OCTETS - 1), :] += jnp.where(row > 5, pltpu.roll(terms[t], 6, 0), 0.0)
                GY[t, k, octet(OCTETS - 1), :] += jnp.where(row > 5, pltpu.roll(grads[t], 6, 0), 0.0)
            return carry

        lax.fori_loop(0, NZ, edge_rows, 0, unroll=16)

    rows_late = ((gy >= n_gy // 2 - 2) & (gy <= n_gy // 2 + 1)) | top

    @pl.when(jnp.logical_not(rows_late))
    def _():
        edge_rows_in()
        prepare(outer)

    quarter = lax.rem(lane, 4)
    level_in_group = (lane // 32).astype(jnp.float32)
    def edge_columns_in(side, first):
        (eastward if side == 0 else westward).wait_recv()
        own = [[packed[4 * t + j] for j in range(4)] for t in range(NT)]
        if side == 0:
            depth = jnp.where(first_half, from_west[5], packed[12])
            fields = [
                [jnp.where(first_half, from_west[j], own[0][j]) for j in range(4)],
                [jnp.where(first_half, pltpu.roll(from_west[j], CX - 2, 1), own[1][j]) for j in range(4)],
            ]
        else:
            depth = jnp.where(first_half, packed[12], from_east[4])
            fields = [
                [jnp.where(first_half, own[0][j], from_east[j]) for j in range(4)],
                [jnp.where(first_half, own[1][j], pltpu.roll(from_east[j], 2, 1)) for j in range(4)],
            ]
        steps = []
        for t in range(NT):
            turned = [pltpu.roll(f, CX - 32, 1) for f in fields[t]]
            steps.append(
                [
                    jnp.where(
                        depth > level_in_group + (4 * j + 1.0),
                        jnp.where(lane < CX - 32, turned[j], turned[min(j + 1, 3)]) - fields[t][j],
                        0.0,
                    )
                    for j in range(4)
                ]
            )
        for j in range(4):
            dz = []
            for t in range(NT):
                before = pltpu.roll(steps[t][j - 1], 32, 1) if j > 0 else zeros
                dz.append(
                    steps[t][j] + jnp.where(lane < 32, before, pltpu.roll(steps[t][j], 32, 1))
                )
            speed = packed[8 + j]
            if side == 0:
                speed = jnp.where(first_half, pltpu.roll(from_west[4], (CX + 1 - j) % CX, 1), speed)
            terms, grads = edge_terms(
                [fields[t][j] for t in range(NT)], dz, depth, speed, level_in_group + 4.0 * j,
                lanes_left, lanes_right,
                None if side == 0 else quarter == 1, quarter == 1 if side == 0 else None,
                None if side == 0 else quarter == 0, quarter == 2 if side == 0 else None,
            )
            for t in range(NT):
                if first:
                    edge_c[t, j] = terms[t]
                    edge_g[t, j] = grads[t]
                else:
                    edge_c[t, j] += terms[t]
                    edge_g[t, j] += grads[t]

    @pl.when(even)
    def _():
        edge_columns_in(1, True)
        edge_columns_in(0, False)

    @pl.when(jnp.logical_not(even))
    def _():
        edge_columns_in(0, True)
        edge_columns_in(1, False)

    at_edge = (lane < 2) | (lane >= CX - 2)

    def finish(octets, prepared):
        def at(o, ref, t, group, b):
            rolled = pltpu.roll(ref[t, group], (CX - (4 * (b * 8 + o) + 2)) % CX, 1)
            return jnp.where(at_edge, rolled, 0.0)

        def body(group, carry):
            fluxes = [[carry[4 * i], carry[4 * i + 1]] for i in range(len(octets))]
            gx_here = [[carry[4 * i + 2], carry[4 * i + 3]] for i in range(len(octets))]
            after = jnp.minimum(group + 1, 3)
            for b in range(4):
                k = 4 * group + b
                level = k.astype(jnp.float32)
                down = jnp.minimum(k + 1, NZ - 1)
                for i, o in enumerate(octets):
                    depth = bf[octet(o), :]
                    here = [T[t, k, octet(o), :] for t in range(NT)]
                    step = [T[t, down, octet(o), :] - here[t] for t in range(NT)]
                    gx_down = [
                        GX[t, down, octet(o), :]
                        + (at(o, edge_g, t, group, b + 1) if b < 3 else at(o, edge_g, t, after, 0))
                        for t in range(NT)
                    ]
                    mean_x = [gx_here[i][t] + gx_down[t] for t in range(NT)]
                    wet = depth > level
                    if prepared:
                        inverse = Q[k, octet(o), :]
                        other = [FY[t, k, octet(o), :] for t in range(NT)]
                        rest = [XY[t, k, octet(o), :] for t in range(NT)]
                    else:
                        mean_y = [
                            GY[t, k, octet(o), :] + GY[t, down, octet(o), :] for t in range(NT)
                        ]
                        inverse = jnp.where(
                            depth > level + 1.0, reciprocal(jnp.maximum(4.0 * density(step), 1.0)), 0.0
                        )
                        slope = jnp.clip(density(mean_y) * inverse, -1.0, 1.0)
                        square = 0.1 * (slope * slope)
                        slope = 0.025 * slope
                        other = [square * step[t] - slope * mean_y[t] for t in range(NT)]
                        rest = [
                            here[t] + (XY[t, k, octet(o), :] + YB[t, k, shifted(o, -1), :])
                            for t in range(NT)
                        ]
                    slope = jnp.clip(density(mean_x) * inverse, -1.0, 1.0)
                    square = 0.1 * (slope * slope)
                    slope = 0.025 * slope
                    for t in range(NT):
                        flux = other[t] + (square * step[t] - slope * mean_x[t])
                        total = (rest[t] + at(o, edge_c, t, group, b)) + (flux - fluxes[i][t])
                        out[t, k, pl.ds(8 * o, 8), :] = jnp.where(wet, total, 0.0)
                        fluxes[i][t] = flux
                    gx_here[i] = gx_down
            return tuple(x for i in range(len(octets)) for x in (*fluxes[i], *gx_here[i]))

        start = []
        for o in octets:
            start += [zeros, zeros]
            start += [GX[t, 0, octet(o), :] + at(o, edge_g, t, 0, 0) for t in range(NT)]
        lax.fori_loop(0, 4, body, tuple(start), unroll=4)

    finish(inner, True)

    @pl.when(rows_late)
    def _():
        edge_rows_in()
        finish(outer, False)

    @pl.when(jnp.logical_not(rows_late))
    def _():
        finish(outer, True)

    eastward.wait_send()
    westward.wait_send()
    pl.when(southward_itself)(lambda: wait_send(southward))
    pl.when(northward_itself)(lambda: wait_send(northward))
    pl.when(relayed_up)(lambda: wait_send(handed_up))
    pl.when(relayed_down)(lambda: wait_send(handed_down))
    pl.when(top)(lambda: wait_send(across))
    pl.when(relays_up)(lambda: wait_send(forwarded_up))
    pl.when(relays_down)(lambda: wait_send(forwarded_down))


def solution(mesh):
    n_gx, n_gy = mesh.shape["gx"], mesh.shape["gy"]
    f32 = jnp.float32
    in_hbm = pl.BlockSpec(memory_space=pltpu.HBM)
    field = pltpu.VMEM((NT, NZ, TALL, CX), f32)
    levels = pltpu.VMEM((NZ, CY, CX), f32)
    plane = pltpu.VMEM((TALL, CX), f32)
    packed = pltpu.VMEM((PACKED, 8, CX), f32)
    eastward = pltpu.VMEM((EASTWARD, 8, CX), f32)
    westward = pltpu.VMEM((WESTWARD, 8, CX), f32)
    edge = pltpu.VMEM((NT, 4, 8, CX), f32)

    def on_device(tracers, east_speed, north_speed, bottom_level):
        return pl.pallas_call(
            functools.partial(kernel, n_gx, n_gy),
            out_shape=jax.ShapeDtypeStruct((NT, NZ, CY, CX), f32),
            in_specs=[in_hbm] * 4,
            out_specs=pl.BlockSpec(memory_space=pltpu.VMEM),
            scratch_shapes=[
                field, levels, levels, pltpu.VMEM((CY, CX), jnp.int32), plane, plane, plane,
                field, field, field, field, field, field, pltpu.VMEM((NZ, TALL, CX), f32),
                packed, eastward, westward, eastward, westward,
                pltpu.VMEM((NT, NZ, 2, CX), f32), pltpu.VMEM((2, CX), jnp.int32),
                pltpu.VMEM((NZ, 1, CX), f32), pltpu.VMEM((FOLD_ROWS, CX), f32),
                pltpu.VMEM((NT, NZ, 8, CX), f32), pltpu.VMEM((8, CX), jnp.int32),
                pltpu.VMEM((NZ, 8, CX), f32), edge, edge,
                pltpu.SemaphoreType.DMA((10,)), pltpu.SemaphoreType.DMA((10,)),
                pltpu.SemaphoreType.DMA((10,)), pltpu.SemaphoreType.REGULAR, pltpu.SemaphoreType.REGULAR,
            ],
            compiler_params=pltpu.CompilerParams(
                collective_id=0, has_side_effects=True, vmem_limit_bytes=24 * 1024 * 1024
            ),
        )(
            *[
                pltpu.with_memory_space_constraint(x, pltpu.HBM)
                for x in (tracers, east_speed, north_speed, bottom_level)
            ]
        )

    in_specs = (P(None, None, "gy", "gx"), P(None, "gy", "gx"), P(None, "gy", "gx"), P("gy", "gx"))
    return jax.shard_map(
        on_device, mesh=mesh, in_specs=in_specs, out_specs=P(None, None, "gy", "gx"), check_vma=False
    )
```

profile of v0, /device:TPU:224, one launch (start us, length us, event | category | flops | bytes accessed | tf_op | source)
XLA Modules:
  0.0 12.3 jit_solution(8386315187177298266)
XLA Ops:
  0.0 11.4 %shard_map.46 = f32[2,16,48,128]{3,2,1,0:T(8,128)S(1)} custom-call(f32[2,16,48,128]{3,2,1,0:T(8,128)} %tracers.1, f32[16,48,128]{2,1,0:T(8,128)} %east.1, f32[16,48,128]{2,1,0:T(8,128)} %north.1, s32[48,128]{1,0:T(8,128)} %bottom.1), custom_call_target="tpu_custom_call" | custom-call | tf_op jit(solution)/shard_map/pallas_call | solution.py:663
  11.4 0.9 %copy.6 = f32[2,16,48,128]{3,2,1,0:T(8,128)} copy(f32[2,16,48,128]{3,2,1,0:T(8,128)S(1)} %shard_map.46) | data formatting | bytes 1572864
where the time goes:
time: 12.4 us; the launch traced here: 12.3 us
  Pallas kernels  11.4 us (92%)
  local copies, waits for them, and re-layouts  0.88 us (7%)
    pallas_call x1, Pallas kernels, on_device(): pl.pallas_call(functools.partial(kernel, n_gx, n_gy), out_shape=jax.Shape...  11.4 us
    unnamed x1, local copies, waits for them, and re-layouts  0.88 us

commit v1 on v0

--- a/solution.py
+++ b/solution.py
@@ -202,6 +202,23 @@
     for copy in early:
         copy.wait()
 
+    @pl.when(top)
+    def _():
+        spots = [(t, k, pl.ds(2 * (NZ * t + k), 2)) for t in range(NT) for k in range(NZ)]
+        for t, k, spot in spots:
+            folded[spot, :] = strip[t, k, OWN_LAST, :]
+        folded[pl.ds(64, 2), :] = strip_b[OWN_LAST, :].astype(jnp.float32)
+        for i in range(FOLD_ROWS // 8):
+            value = folded[pl.ds(8 * i, 8), :]
+            for bit in (64, 32, 16, 8, 4, 2, 1):
+                value = jnp.where(
+                    (lane & bit) != 0, pltpu.roll(value, bit, 1), pltpu.roll(value, CX - bit, 1)
+                )
+            folded[pl.ds(8 * i, 8), :] = jnp.where((row & 1) != 0, rows_down(value), rows_up(value))
+        for t, k, spot in spots:
+            relay[t, k] = folded[spot, :]
+        relay_b[...] = folded[pl.ds(64, 2), :].astype(jnp.int32)
+
     def send(source, target, index, slot, device):
         return pltpu.make_async_remote_copy(
             src_ref=source, dst_ref=target, send_sem=send_sem.at[index], recv_sem=recv_sem.at[slot],
@@ -233,7 +250,7 @@
     between = [relay, relay_b, relay_v]
     northward = bundle(last, from_south, 2, 2, north_id)
     southward = bundle(first, from_north, 5, 5, south_id)
-    across = bundle(last[:2], from_north, 2, 5, mirror_id)
+    across = bundle(between[:2], from_north, 2, 5, mirror_id)
     handed_up = bundle(last, between, 2, 7, (chip_mate, gy))
     handed_down = bundle(first, between[:2], 5, 7, (chip_mate, gy))
     forwarded_up = bundle(between, from_south, 7, 2, (chip_mate, gy + 1))
@@ -257,12 +274,13 @@
 
         pl.when(relayed_up)(lambda: start(handed_up))
 
+        pl.when(northward_itself & below_middle)(lambda: start(northward))
+
         @pl.when(relays_up)
         def _():
             wait_recv(handed_up)
             start(forwarded_up)
 
-        pl.when(northward_itself & below_middle)(lambda: start(northward))
         pl.when(relayed_down)(lambda: start(handed_down))
         pl.when(southward_itself & jnp.logical_not(relays_down))(lambda: start(southward))
         pl.when(northward_itself & jnp.logical_not(below_middle | above_middle))(lambda: start(northward))
@@ -441,32 +459,6 @@
     def edge_rows_in():
         wait_recv(southward)
         pl.when(jnp.logical_not(base))(lambda: wait_recv(northward))
-
-        @pl.when(top)
-        def _():
-            def gather(k, carry):
-                for t in range(NT):
-                    folded[pl.ds(2 * (NZ * t + k), 2), :] = strip[t, k, FROM_NORTH, :]
-                return carry
-
-            def scatter(k, carry):
-                for t in range(NT):
-                    strip[t, k, FROM_NORTH, :] = folded[pl.ds(2 * (NZ * t + k), 2), :]
-                return carry
-
-            lax.fori_loop(0, NZ, gather, 0, unroll=4)
-            folded[pl.ds(64, 8), :] = strip_b[...].astype(jnp.float32)
-            for i in range(FOLD_ROWS // 8):
-                value = folded[pl.ds(8 * i, 8), :]
-                for bit in (64, 32, 16, 8, 4, 2, 1):
-                    value = jnp.where(
-                        (lane & bit) != 0, pltpu.roll(value, bit, 1), pltpu.roll(value, CX - bit, 1)
-                    )
-                folded[pl.ds(8 * i, 8), :] = jnp.where(
-                    (row & 1) != 0, rows_down(value), rows_up(value)
-                )
-            lax.fori_loop(0, NZ, scatter, 0, unroll=4)
-            strip_b[FROM_NORTH, :] = folded[pl.ds(66, 2), :].astype(jnp.int32)
 
         def edge_rows(k, carry):
             level = k.astype(jnp.float32)

time: 12.4 us -> 12.3 us (level)
  the two profiles are of different devices: /device:TPU:224 before, /device:TPU:24 now
where the time goes in v1:
time: 12.3 us; the launch traced here: 12.1 us
  Pallas kernels  11.2 us (91%)
  local copies, waits for them, and re-layouts  0.88 us (7%)
    pallas_call x1, Pallas kernels, on_device(): pl.pallas_call(functools.partial(kernel, n_gx, n_gy), out_shape=jax.Shape...  11.2 us
    unnamed x1, local copies, waits for them, and re-layouts  0.88 us

profile of v1, /device:TPU:24, one launch (start us, length us, event | category | flops | bytes accessed | tf_op | source)
XLA Modules:
  0.0 12.1 jit_solution(7690095536726401633)
XLA Ops:
  0.0 11.2 %shard_map.46 = f32[2,16,48,128]{3,2,1,0:T(8,128)S(1)} custom-call(f32[2,16,48,128]{3,2,1,0:T(8,128)} %tracers.1, f32[16,48,128]{2,1,0:T(8,128)} %east.1, f32[16,48,128]{2,1,0:T(8,128)} %north.1, s32[48,128]{1,0:T(8,128)} %bottom.1), custom_call_target="tpu_custom_call" | custom-call | tf_op jit(solution)/shard_map/pallas_call | solution.py:655
  11.2 0.9 %copy.6 = f32[2,16,48,128]{3,2,1,0:T(8,128)} copy(f32[2,16,48,128]{3,2,1,0:T(8,128)S(1)} %shard_map.46) | data formatting | bytes 1572864

commit v2 on v1

--- a/solution.py
+++ b/solution.py
@@ -274,13 +274,12 @@
 
         pl.when(relayed_up)(lambda: start(handed_up))
 
-        pl.when(northward_itself & below_middle)(lambda: start(northward))
-
         @pl.when(relays_up)
         def _():
             wait_recv(handed_up)
             start(forwarded_up)
 
+        pl.when(northward_itself & below_middle)(lambda: start(northward))
         pl.when(relayed_down)(lambda: start(handed_down))
         pl.when(southward_itself & jnp.logical_not(relays_down))(lambda: start(southward))
         pl.when(northward_itself & jnp.logical_not(below_middle | above_middle))(lambda: start(northward))
@@ -586,28 +585,24 @@
                         other = [FY[t, k, octet(o), :] for t in range(NT)]
                         rest = [XY[t, k, octet(o), :] for t in range(NT)]
                     else:
-                        mean_y = [
-                            GY[t, k, octet(o), :] + GY[t, down, octet(o), :] for t in range(NT)
-                        ]
                         inverse = jnp.where(
                             depth > level + 1.0, reciprocal(jnp.maximum(4.0 * density(step), 1.0)), 0.0
                         )
-                        slope = jnp.clip(density(mean_y) * inverse, -1.0, 1.0)
-                        square = 0.1 * (slope * slope)
-                        slope = 0.025 * slope
-                        other = [square * step[t] - slope * mean_y[t] for t in range(NT)]
-                        rest = [
-                            here[t] + (XY[t, k, octet(o), :] + YB[t, k, shifted(o, -1), :])
-                            for t in range(NT)
-                        ]
+                        Q[k, octet(o), :] = inverse
                     slope = jnp.clip(density(mean_x) * inverse, -1.0, 1.0)
                     square = 0.1 * (slope * slope)
                     slope = 0.025 * slope
                     for t in range(NT):
-                        flux = other[t] + (square * step[t] - slope * mean_x[t])
-                        total = (rest[t] + at(o, edge_c, t, group, b)) + (flux - fluxes[i][t])
-                        out[t, k, pl.ds(8 * o, 8), :] = jnp.where(wet, total, 0.0)
-                        fluxes[i][t] = flux
+                        flux = square * step[t] - slope * mean_x[t]
+                        term = at(o, edge_c, t, group, b)
+                        if prepared:
+                            flux = other[t] + flux
+                            total = (rest[t] + term) + (flux - fluxes[i][t])
+                            out[t, k, pl.ds(8 * o, 8), :] = jnp.where(wet, total, 0.0)
+                            fluxes[i][t] = flux
+                        else:
+                            FY[t, k, octet(o), :] = flux
+                            XY[t, k, octet(o), :] += term + (here[t] + YB[t, k, shifted(o, -1), :])
                     gx_here[i] = gx_down
             return tuple(x for i in range(len(octets)) for x in (*fluxes[i], *gx_here[i]))
 
@@ -619,10 +614,36 @@
 
     finish(inner, True)
 
+    def finish_rows(octets):
+        def body(k, carry):
+            level = k.astype(jnp.float32)
+            down = jnp.minimum(k + 1, NZ - 1)
+            fluxes, gy_down = [], []
+            for i, o in enumerate(octets):
+                inverse = Q[k, octet(o), :]
+                wet = bf[octet(o), :] > level
+                below = [GY[t, down, octet(o), :] for t in range(NT)]
+                mean_y = [carry[1][NT * i + t] + below[t] for t in range(NT)]
+                slope = jnp.clip(density(mean_y) * inverse, -1.0, 1.0)
+                square = 0.1 * (slope * slope)
+                slope = 0.025 * slope
+                for t in range(NT):
+                    step = T[t, down, octet(o), :] - T[t, k, octet(o), :]
+                    flux = FY[t, k, octet(o), :] + (square * step - slope * mean_y[t])
+                    total = XY[t, k, octet(o), :] + (flux - carry[0][NT * i + t])
+                    out[t, k, pl.ds(8 * o, 8), :] = jnp.where(wet, total, 0.0)
+                    fluxes.append(flux)
+                gy_down += below
+            return tuple(fluxes), tuple(gy_down)
+
+        top_gy = tuple(GY[t, 0, octet(o), :] for o in octets for t in range(NT))
+        lax.fori_loop(0, NZ, body, (tuple(zeros for _ in top_gy), top_gy), unroll=16)
+
     @pl.when(rows_late)
     def _():
+        finish(outer, False)
         edge_rows_in()
-        finish(outer, False)
+        finish_rows(outer)
 
     @pl.when(jnp.logical_not(rows_late))
     def _():

time: 12.3 us -> 12.2 us (level); the launches traced: 12.1 us -> 12.1 us
  no operation moved by 1% of the time
where the time goes in v2:
time: 12.2 us; the launch traced here: 12.1 us
  Pallas kernels  11.2 us (92%)
  local copies, waits for them, and re-layouts  0.88 us (7%)
    pallas_call x1, Pallas kernels, on_device(): pl.pallas_call(functools.partial(kernel, n_gx, n_gy), out_shape=jax.Shape...  11.2 us
    unnamed x1, local copies, waits for them, and re-layouts  0.88 us

profile of v2, /device:TPU:24, one launch (start us, length us, event | category | flops | bytes accessed | tf_op | source)
XLA Modules:
  0.0 12.1 jit_solution(7324587324586670682)
XLA Ops:
  0.0 11.2 %shard_map.46 = f32[2,16,48,128]{3,2,1,0:T(8,128)S(1)} custom-call(f32[2,16,48,128]{3,2,1,0:T(8,128)} %tracers.1, f32[16,48,128]{2,1,0:T(8,128)} %east.1, f32[16,48,128]{2,1,0:T(8,128)} %north.1, s32[48,128]{1,0:T(8,128)} %bottom.1), custom_call_target="tpu_custom_call" | custom-call | tf_op jit(solution)/shard_map/pallas_call | solution.py:676
  11.3 0.9 %copy.6 = f32[2,16,48,128]{3,2,1,0:T(8,128)} copy(f32[2,16,48,128]{3,2,1,0:T(8,128)S(1)} %shard_map.46) | data formatting | bytes 1572864

commit v3 on v2

--- a/solution.py
+++ b/solution.py
@@ -150,9 +150,7 @@
     )
 
     def load(source, target, index):
-        copy = pltpu.make_async_copy(source, target, load_sem.at[index])
-        copy.start()
-        return copy
+        return pltpu.make_async_copy(source, target, load_sem.at[index])
 
     last_rows, first_rows = pl.ds(CY - 2, 2), pl.ds(0, 2)
     early = [
@@ -169,6 +167,18 @@
         load(east, U, 8),
         load(north, V, 9),
     ]
+
+    bulk_first = before_seam & (gy < n_gy // 2 - 1)
+
+    @pl.when(bulk_first)
+    def _():
+        for copy in late[:3] + early + late[3:]:
+            copy.start()
+
+    @pl.when(jnp.logical_not(bulk_first))
+    def _():
+        for copy in early + late:
+            copy.start()
 
     lane = lax.broadcasted_iota(jnp.int32, (8, CX), 1)
     row = lax.broadcasted_iota(jnp.int32, (8, CX), 0)
@@ -483,7 +493,9 @@
 
         lax.fori_loop(0, NZ, edge_rows, 0, unroll=16)
 
-    rows_late = ((gy >= n_gy // 2 - 2) & (gy <= n_gy // 2 + 1)) | top
+    rows_late = ((gy >= n_gy // 2 - 1) & (gy <= n_gy // 2 + 1)) | top | (
+        (gy == n_gy // 2 - 2) & jnp.logical_not(crosses_up)
+    )
 
     @pl.when(jnp.logical_not(rows_late))
     def _():

time: 12.2 us -> 12.2 us (level)
  no operation moved by 1% of the time
where the time goes in v3:
time: 12.2 us
  Pallas kernels  11.3 us (93%)
  local copies, waits for them, and re-layouts  0.88 us (7%)
    pallas_call x1, Pallas kernels, on_device(): pl.pallas_call(functools.partial(kernel, n_gx, n_gy), out_shape=jax.Shape...  11.3 us
    unnamed x1, local copies, waits for them, and re-layouts  0.88 us

profile of v3, /device:TPU:24, one launch (start us, length us, event | category | flops | bytes accessed | tf_op | source)
XLA Modules:
  0.0 12.2 jit_solution(4190812794415924828)
XLA Ops:
  0.0 11.3 %shard_map.46 = f32[2,16,48,128]{3,2,1,0:T(8,128)S(1)} custom-call(f32[2,16,48,128]{3,2,1,0:T(8,128)} %tracers.1, f32[16,48,128]{2,1,0:T(8,128)} %east.1, f32[16,48,128]{2,1,0:T(8,128)} %north.1, s32[48,128]{1,0:T(8,128)} %bottom.1), custom_call_target="tpu_custom_call" | custom-call | tf_op jit(solution)/shard_map/pallas_call | solution.py:688
  11.3 0.9 %copy.6 = f32[2,16,48,128]{3,2,1,0:T(8,128)} copy(f32[2,16,48,128]{3,2,1,0:T(8,128)S(1)} %shard_map.46) | data formatting | bytes 1572864
